TPU v7x, 32 devices: a whole 2x2x4 slice. The times are simulated.
32 devices in a mesh: win: 2 (over y), tmpl: 4 (over z), sta: 4 (over x, core).
Axes of the slice: x: 2, y: 2, z: 4, core: 2. Of those that a mesh axis runs over, the one named last changes fastest.
Arguments:
- records: bfloat16 [384, 3, 3584], P(('win', 'sta')), parts along dimension 0
- templates: bfloat16 [16, 192, 3, 100], P(('win', 'tmpl'), 'sta'), parts along dimension 0
- channel_valid: int32 [16, 192, 3], P(('win', 'tmpl'), 'sta'), parts along dimension 0, may hold values from 0 to 1, as said below
- shifts: int32 [16, 192], P(('win', 'tmpl'), 'sta'), parts along dimension 0, may hold values from 0 to 412, as said below
- hypo_id: int32 [16], P(('win', 'tmpl')), parts along dimension 0, may hold values from 0 to 255
- hypo_xyz: float32 [3, 256], replicated, may hold values from -1 to 1
Outputs:
- peak_score: float32 [6144], P(('win', 'sta')), parts along dimension 0
- evidence: float32 [6144], P(('win', 'sta')), parts along dimension 0
- location: float32 [3, 6144], P(None, ('win', 'sta')), parts along dimension 1
There are 2 independent parts, one for each index of `win`. A program takes and returns all parts, laid end to end along the dimension named above; an argument that names none is the same for every part. Nothing has to cross between parts.
Inputs may be any that keep to these rules, and one draw needn't show every extreme that they name: `channel_valid`: every template has all three channels of at least one station valid. `shifts`: for every template some station has moveout 0.
All inputs are finite; a program needn't handle non-finite values.
Results may differ from a plain program's by a relative error of at most 0.0044.
Values sent between devices are 32-bit elements; how exact they have to be, the bound alone decides.
A program may use at most 64 MiB of HBM per device.

v0:
```python
import functools
import math

import jax
import jax.numpy as jnp
from jax import lax
from jax.experimental import pallas as pl
from jax.experimental.pallas import tpu as pltpu
from jax.sharding import PartitionSpec as P

SAMPLES = 3072

sharpness = 400.0
epsilon = 1e-06
LANES = 128


def trace_kernel(
    taps, group, unroll, shift_ref, valid_ref, hypo_ref, place_ref, x_ref, w_ref,
    out_ref, xs, xw, rn, ws, acc, scr
):
    comps, stations, samples = x_ref.shape
    chunks, temps, chunk_rows = out_ref.shape[:3]
    out_rows = acc.shape[1]
    rows = samples // LANES
    prows = -(-(rows + 1) // 8) * 8
    srows = comps * prows
    j_id = lax.broadcasted_iota(jnp.int32, (LANES, LANES), 0)
    i_id = lax.broadcasted_iota(jnp.int32, (LANES, LANES), 1)
    upper = j_id >= i_id
    gap = j_id - i_id
    band = jnp.concatenate(
        [
            jnp.where((gap >= 0) & (gap < taps), 1.0, 0.0),
            jnp.where(gap + LANES < taps, 1.0, 0.0),
        ],
        axis=0,
    ).astype(jnp.bfloat16)

    k_id = lax.broadcasted_iota(jnp.int32, (taps, LANES), 0)
    l_id = lax.broadcasted_iota(jnp.int32, (taps, LANES), 1)
    turn = jnp.where(lax.bitwise_and(k_id + l_id, LANES - 1) == 0, 1.0, 0.0).astype(jnp.bfloat16)
    for c in range(comps):
        for t in range(temps):
            wide = w_ref[t, c].astype(jnp.float32)
            power = jnp.sum(wide * wide, axis=-1, keepdims=True) / taps
            normed = (wide / (taps * jnp.sqrt(power + epsilon))).astype(jnp.bfloat16)
            ws[pl.ds((c * temps + t) * stations, stations), :] = jnp.dot(
                normed, turn, preferred_element_type=jnp.float32
            )

    xs[pl.ds(stations * srows, 8), :] = jnp.zeros((8, LANES), jnp.float32)

    def prepare(g, _):
        base = pl.multiple_of(g * (group * srows), 8)
        first = pl.multiple_of(g * group, group)
        for k in range(group * comps):
            xs[pl.ds(base + k * prows + prows - 8, 8), :] = jnp.zeros((8, LANES), jnp.float32)
        for c in range(comps):
            wave = x_ref[c, pl.ds(first, group), :].astype(jnp.float32)
            for r in range(rows):
                xs[pl.ds(base + c * prows + r, group, stride=srows), :] = wave[
                    :, r * LANES : (r + 1) * LANES
                ]
        count = group * srows
        here = xs[pl.ds(base, count), :]
        after = xs[pl.ds(base + 1, count), :]
        window = jnp.concatenate([here, after], axis=1)
        xw[pl.ds(base, count), :] = window.astype(jnp.bfloat16)
        square = window * window
        high = square.astype(jnp.bfloat16)
        low = (square - high.astype(jnp.float32)).astype(jnp.bfloat16)
        energy = jnp.dot(high, band, preferred_element_type=jnp.float32) + jnp.dot(
            low, band, preferred_element_type=jnp.float32
        )
        rn[pl.ds(base, count), :] = lax.rsqrt(energy * (1.0 / taps) + epsilon)
        return 0

    lax.fori_loop(0, stations // group, prepare, 0)

    lane = lax.broadcasted_iota(jnp.int32, (out_rows, LANES), 1)

    def one_station(s, slot, counts):
        sums = [None] * temps
        counts = list(counts)
        for c in range(comps):
            base = pl.multiple_of((s * comps + c) * prows, 16)
            data = xw[pl.ds(base, prows), :]
            inverse = rn[pl.ds(base, prows), :]
            tiles = []
            for t in range(temps):
                valid = valid_ref[c, t, s]
                counts[t] = counts[t] + valid
                row = ws[pl.ds((c * temps + t) * stations + s, 1), :] * valid.astype(jnp.float32)
                ring = pltpu.roll(
                    jnp.broadcast_to(row, (LANES, LANES)), 0, 1, stride=1, stride_axis=0
                )
                tiles.append(
                    jnp.concatenate(
                        [jnp.where(upper, ring, 0.0), jnp.where(upper, 0.0, ring)], axis=0
                    ).astype(jnp.bfloat16)
                )
            raw = jnp.dot(
                data, jnp.concatenate(tiles, axis=1), preferred_element_type=jnp.float32
            )
            for t in range(temps):
                term = raw[:, t * LANES : (t + 1) * LANES] * inverse
                sums[t] = term if sums[t] is None else sums[t] + term
        for t in range(temps):
            shift = shift_ref[t, s]
            whole = lax.shift_right_logical(shift, 7)
            part = lax.bitwise_and(shift, LANES - 1)
            scr[slot, t] = pltpu.roll(
                sums[t], lax.bitwise_and(LANES - part, LANES - 1), 1
            )
            near = scr[slot, t, pl.ds(whole, out_rows), :]
            far = scr[slot, t, pl.ds(whole + 1, out_rows), :]
            acc[t] += jnp.where(lane < LANES - part, near, far)
        return tuple(counts)

    acc[...] = jnp.zeros_like(acc)

    def some_stations(g, counts):
        for k in range(unroll):
            counts = one_station(g * unroll + k, k, counts)
        return counts

    counts = lax.fori_loop(
        0, stations // unroll, some_stations, tuple(jnp.int32(0) for _ in range(temps))
    )

    share = out_rows // chunks
    axes, hypos = place_ref.shape
    h_id = lax.broadcasted_iota(jnp.int32, (axes, hypos), 1)
    row_id = lax.broadcasted_iota(jnp.int32, (axes, LANES), 0)
    col_id = lax.broadcasted_iota(jnp.int32, (axes, LANES), 1)
    for t in range(temps):
        place = jnp.sum(
            jnp.where(h_id == hypo_ref[t], place_ref[...], 0.0), axis=1, keepdims=True
        )
        place_row = jnp.sum(jnp.where(row_id == col_id, place, 0.0), axis=0, keepdims=True)
        count_row = jnp.full((1, LANES), counts[t].astype(jnp.float32))
        for b in range(chunks):
            out_ref[b, t, pl.ds(0, share), :] = acc[t, pl.ds(b * share, share), :]
            out_ref[b, t, pl.ds(share, 1), :] = count_row
            out_ref[b, t, pl.ds(share + 1, 1), :] = place_row
            if chunk_rows > share + 2:
                out_ref[b, t, pl.ds(share + 2, chunk_rows - share - 2), :] = jnp.zeros(
                    (chunk_rows - share - 2, LANES), jnp.float32
                )


def partial_traces(records, templates, channel_valid, shifts, hypo_id, hypo_xyz):
    stations, comps, samples = records.shape
    temps, taps = templates.shape[0], templates.shape[-1]
    rows = samples // LANES
    prows = -(-(rows + 1) // 8) * 8
    total = stations * comps * prows
    group = math.gcd(stations, 16)
    unroll = math.gcd(stations, 2)
    chunks = lax.axis_size("sta")
    out_rows = SAMPLES // LANES
    chunk_rows = -(-(out_rows // chunks + 2) // 8) * 8
    smem = pl.BlockSpec(memory_space=pltpu.SMEM)
    vmem = pl.BlockSpec(memory_space=pltpu.VMEM)
    return pl.pallas_call(
        functools.partial(trace_kernel, taps, group, unroll),
        out_shape=jax.ShapeDtypeStruct((chunks, temps, chunk_rows, LANES), jnp.float32),
        in_specs=[smem, smem, smem, vmem, vmem, vmem],
        out_specs=vmem,
        scratch_shapes=[
            pltpu.VMEM((total + 8, LANES), jnp.float32),
            pltpu.VMEM((total, 2 * LANES), jnp.bfloat16),
            pltpu.VMEM((total, LANES), jnp.float32),
            pltpu.VMEM((comps * temps * stations, LANES), jnp.float32),
            pltpu.VMEM((temps, out_rows, LANES), jnp.float32),
            pltpu.VMEM((unroll, temps, prows, LANES), jnp.float32),
        ],
        compiler_params=pltpu.CompilerParams(vmem_limit_bytes=40 * 2**20),
        name="traces",
    )(
        shifts,
        jnp.transpose(channel_valid, (2, 0, 1)),
        hypo_id,
        hypo_xyz,
        jnp.transpose(records, (1, 0, 2)),
        jnp.transpose(templates, (0, 2, 1, 3)),
    )


def combine_kernel(
    share, axes, n_sta, n_tmpl, part_ref, best_ref, evidence_ref, place_ref,
    summed, held, score_held, send_a, recv_a, send_b, recv_b
):
    temps = part_ref.shape[1]
    sta, tmpl = lax.axis_index("sta"), lax.axis_index("tmpl")
    barrier = pltpu.get_barrier_semaphore()
    for k in range(1, n_sta):
        pl.semaphore_signal(
            barrier, inc=1, device_id={"sta": lax.rem(sta + k, n_sta)},
            device_id_type=pl.DeviceIdType.MESH,
        )
    for k in range(1, n_tmpl):
        pl.semaphore_signal(
            barrier, inc=1, device_id={"tmpl": lax.rem(tmpl + k, n_tmpl)},
            device_id_type=pl.DeviceIdType.MESH,
        )
    pl.semaphore_wait(barrier, n_sta + n_tmpl - 2)

    copies = []
    for k in range(1, n_sta):
        peer = lax.rem(sta + k, n_sta)
        copies.append(
            pltpu.make_async_remote_copy(
                src_ref=part_ref.at[peer],
                dst_ref=held.at[k - 1],
                send_sem=send_a.at[k - 1],
                recv_sem=recv_a.at[k - 1],
                device_id={"sta": peer},
                device_id_type=pl.DeviceIdType.MESH,
            )
        )
        copies[-1].start()
    whole = part_ref[sta]
    for k, copy in enumerate(copies):
        copy.wait_recv()
        whole = whole + held[k]
    row_id = lax.broadcasted_iota(jnp.int32, whole.shape, 1)
    counts = whole[:, share : share + 1, :]
    summed[...] = jnp.where(
        row_id < share, sharpness * (whole / counts), part_ref[sta]
    )
    later = []
    for k in range(1, n_tmpl):
        peer = lax.rem(tmpl + k, n_tmpl)
        later.append(
            pltpu.make_async_remote_copy(
                src_ref=summed,
                dst_ref=score_held.at[k - 1],
                send_sem=send_b.at[k - 1],
                recv_sem=recv_b.at[k - 1],
                device_id={"tmpl": peer},
                device_id_type=pl.DeviceIdType.MESH,
            )
        )
        later[-1].start()
    for copy in copies:
        copy.wait_send()
    blocks = [summed[...]]
    for k, copy in enumerate(later):
        copy.wait_recv()
        blocks.append(score_held[k])
    pieces = [block[t] for block in blocks for t in range(temps)]
    best = pieces[0]
    for piece in pieces[1:]:
        best = jnp.maximum(best, piece)
    total = jnp.zeros_like(best)
    sums = [jnp.zeros_like(best) for _ in range(axes)]
    for piece in pieces:
        weight = jnp.exp(piece - best)
        total = total + weight
        for j in range(axes):
            sums[j] = sums[j] + weight * piece[share + 1 : share + 2, j : j + 1]
    best_ref[...] = best[:share]
    evidence_ref[...] = (best + jnp.log(total))[:share]
    for j in range(axes):
        located = sums[j] / total
        for r in range(share):
            place_ref[pl.ds(j, 1), pl.ds(r * LANES, LANES)] = located[r : r + 1]
    for copy in later:
        copy.wait_send()


def on_device(records, templates, channel_valid, shifts, hypo_id, hypo_xyz):
    part = partial_traces(records, templates, channel_valid, shifts, hypo_id, hypo_xyz)
    n_sta, n_tmpl = lax.axis_size("sta"), lax.axis_size("tmpl")
    axes = hypo_xyz.shape[0]
    block = part.shape[1:]
    share = SAMPLES // LANES // n_sta
    vmem = pl.BlockSpec(memory_space=pltpu.VMEM)
    best, evidence, location = pl.pallas_call(
        functools.partial(combine_kernel, share, axes, n_sta, n_tmpl),
        out_shape=(
            jax.ShapeDtypeStruct((share, LANES), jnp.float32),
            jax.ShapeDtypeStruct((share, LANES), jnp.float32),
            jax.ShapeDtypeStruct((axes, share * LANES), jnp.float32),
        ),
        in_specs=[vmem],
        out_specs=(vmem, vmem, vmem),
        scratch_shapes=[
            pltpu.VMEM(block, jnp.float32),
            pltpu.VMEM((n_sta - 1,) + block, jnp.float32),
            pltpu.VMEM((n_tmpl - 1,) + block, jnp.float32),
            pltpu.SemaphoreType.DMA((n_sta - 1,)),
            pltpu.SemaphoreType.DMA((n_sta - 1,)),
            pltpu.SemaphoreType.DMA((n_tmpl - 1,)),
            pltpu.SemaphoreType.DMA((n_tmpl - 1,)),
        ],
        compiler_params=pltpu.CompilerParams(collective_id=0, has_side_effects=True),
        name="combine",
    )(part)
    return (best.reshape(-1), evidence.reshape(-1), location)


def solution(mesh):
    return jax.shard_map(
        on_device,
        mesh=mesh,
        in_specs=(
            P(("win", "sta"), None, None),
            P(("win", "tmpl"), "sta", None, None),
            P(("win", "tmpl"), "sta", None),
            P(("win", "tmpl"), "sta"),
            P(("win", "tmpl")),
            P(),
        ),
        out_specs=(P(("win", "sta")), P(("win", "sta")), P(None, ("win", "sta"))),
        check_vma=False,
    )
```

profile of v0, /device:TPU:0, one launch (start us, length us, event | category | flops | bytes accessed | tf_op | source)
XLA Modules:
  0.0 33.4 jit_solution(17470383228228633831)
XLA Ops:
  0.6 0.0 copy-start.3
  0.6 0.0 copy-start.5
  0.7 0.0 copy-start.6
  0.7 0.7 %copy-done.3 = f32[3,256]{1,0:T(4,128)S(1)} copy-done((f32[3,256]{1,0:T(4,128)S(1)}, f32[3,256]{1,0:T(4,128)}, u32[]{:S(2)}) %copy-start.3) | copy-done | bytes 3096
  1.3 0.0 copy-done.5
  1.3 0.0 copy-done.6
  1.3 0.0 copy-start
  1.3 1.2 %copy-done = bf16[48,3,3584]{2,0,1:T(8,128)(2,1)S(1)} copy-done((bf16[48,3,3584]{2,0,1:T(8,128)(2,1)S(1)}, bf16[48,3,3584]{2,0,1:T(8,128)(2,1)}, u32[]{:S(2)}) %copy-start) | copy-done | bytes 1032216
  2.6 0.0 copy-start.2
  2.6 0.9 %copy-done.2 = bf16[2,48,3,100]{3,1,2,0:T(8,128)(2,1)S(1)} copy-done((bf16[2,48,3,100]{3,1,2,0:T(8,128)(2,1)S(1)}, bf16[2,48,3,100]{3,1,2,0:T(8,128)(2,1)}, u32[]{:S(2)}) %copy-start.2) | copy-done | bytes 57624
  3.4 0.7 %copy-done.4 = s32[2,48,3]{1,0,2:T(2,128)S(1)} copy-done((s32[2,48,3]{1,0,2:T(2,128)S(1)}, s32[2,48,3]{1,0,2:T(2,128)}, u32[]{:S(2)}) %copy-start.4) | copy-done | bytes 1176
  4.1 14.0 %traces.1.part_ref = f32[4,2,8,128]{3,2,1,0:T(8,128)S(1)} custom-call(s32[2,48]{1,0:T(2,128)S(1)} %copy-done.5, s32[3,2,48]{2,1,0:T(2,128)S(1)} %bitcast.7, s32[2]{0:T(128)S(1)} %copy-done.6, f32[3,256]{1,0:T(4,128)S(1)} %copy-done.3, bf16[3,48,3584]{2,1,0:T(8,128)(2,1)S(1)} %bitcast.5, bf16[2,3,48,100]{3,2,1,0:T(8,128)(2,1)S(1)} %bitcast.6), custom_call_target="tpu_custom_call" | custom-call | tf_op jit(solution)/shard_map/traces/pallas_call | solution.py:166
  18.2 0.0 copy-start.1
  18.2 0.6 %copy-done.1 = f32[4,2,8,128]{3,2,1,0:T(8,128)} copy-done((f32[4,2,8,128]{3,2,1,0:T(8,128)}, f32[4,2,8,128]{3,2,1,0:T(8,128)S(1)}, u32[]{:S(2)}) %copy-start.1) | copy-done | bytes 32792
  18.8 12.1 %combine.1 = (f32[6,128]{1,0:T(8,128)}, f32[6,128]{1,0:T(8,128)}, f32[3,768]{1,0:T(4,128)}) custom-call(f32[4,2,8,128]{3,2,1,0:T(8,128)} %copy-done.1), custom_call_target="tpu_custom_call" | custom-call | tf_op jit(solution)/shard_map/combine/pallas_call | solution.py:281
  30.9 0.0 copy-start.9
  30.9 0.0 copy-start.8
  30.9 0.0 copy-start.7
  30.9 0.6 %copy-done.9 = f32[6,128]{1,0:T(8,128)S(1)} copy-done((f32[6,128]{1,0:T(8,128)S(1)}, f32[6,128]{1,0:T(8,128)}, u32[]{:S(2)}) %copy-start.9) | copy-done | bytes 3096
  31.6 0.6 %copy.12 = f32[768]{0:T(1024)} copy(f32[768]{0:T(1024)S(1)} %bitcast.9) | data formatting | bytes 6144
  32.2 0.0 copy-done.8
  32.2 0.6 %copy.13 = f32[768]{0:T(1024)} copy(f32[768]{0:T(1024)S(1)} %bitcast.8) | data formatting | bytes 6144
  32.8 0.0 copy-done.7
  32.8 0.6 %copy.14 = f32[3,768]{1,0:T(4,128)} copy(f32[3,768]{1,0:T(4,128)S(1)} %copy-done.7) | data formatting | bytes 18432
  (1 shorter events, 0.0 us)
Async XLA Ops:
  0.6 0.7 %copy-start.3 = (f32[3,256]{1,0:T(4,128)S(1)}, f32[3,256]{1,0:T(4,128)}, u32[]{:S(2)}) copy-start(f32[3,256]{1,0:T(4,128)} %place_ref.1) | copy-start | bytes 9220
  0.6 0.7 %copy-start.5 = (s32[2,48]{1,0:T(2,128)S(1)}, s32[2,48]{1,0:T(2,128)}, u32[]{:S(2)}) copy-start(s32[2,48]{1,0:T(2,128)} %shift_ref.1) | copy-start | bytes 1156
  0.7 0.7 %copy-start.6 = (s32[2]{0:T(128)S(1)}, s32[2]{0:T(128)}, u32[]{:S(2)}) copy-start(s32[2]{0:T(128)} %hypo_ref.1) | copy-start | bytes 28
  1.3 1.2 %copy-start = (bf16[48,3,3584]{2,0,1:T(8,128)(2,1)S(1)}, bf16[48,3,3584]{2,0,1:T(8,128)(2,1)}, u32[]{:S(2)}) copy-start(bf16[48,3,3584]{2,0,1:T(8,128)(2,1)} %param.6) | copy-start | bytes 3096580
  2.6 0.9 %copy-start.2 = (bf16[2,48,3,100]{3,1,2,0:T(8,128)(2,1)S(1)}, bf16[2,48,3,100]{3,1,2,0:T(8,128)(2,1)}, u32[]{:S(2)}) copy-start(bf16[2,48,3,100]{3,1,2,0:T(8,128)(2,1)} %param.7) | copy-start | bytes 172804
  3.4 0.7 %copy-start.4 = (s32[2,48,3]{1,0,2:T(2,128)S(1)}, s32[2,48,3]{1,0,2:T(2,128)}, u32[]{:S(2)}) copy-start(s32[2,48,3]{1,0,2:T(2,128)} %param.8) | copy-start | bytes 3460
  18.2 0.6 %copy-start.1 = (f32[4,2,8,128]{3,2,1,0:T(8,128)}, f32[4,2,8,128]{3,2,1,0:T(8,128)S(1)}, u32[]{:S(2)}) copy-start(f32[4,2,8,128]{3,2,1,0:T(8,128)S(1)} %traces.1.part_ref) | copy-start | bytes 98308
  30.9 0.7 %copy-start.9 = (f32[6,128]{1,0:T(8,128)S(1)}, f32[6,128]{1,0:T(8,128)}, u32[]{:S(2)}) copy-start(f32[6,128]{1,0:T(8,128)} %get-tuple-element.6) | copy-start | bytes 9220
  30.9 1.3 %copy-start.8 = (f32[6,128]{1,0:T(8,128)S(1)}, f32[6,128]{1,0:T(8,128)}, u32[]{:S(2)}) copy-start(f32[6,128]{1,0:T(8,128)} %get-tuple-element.7) | copy-start | bytes 9220
  30.9 1.8 %copy-start.7 = (f32[3,768]{1,0:T(4,128)S(1)}, f32[3,768]{1,0:T(4,128)}, u32[]{:S(2)}) copy-start(f32[3,768]{1,0:T(4,128)} %get-tuple-element.14) | copy-start | bytes 27652
where the time goes:
time: 33.7 us; the launch traced here: 33.4 us
  Pallas kernels  26.1 us (77%)
  local copies, waits for them, and re-layouts  6.51 us (19%)
  between operations  0.71 us (2%)
    pallas_call x1, Pallas kernels, partial_traces(): pl.pallas_call(functools.partial(trace_kernel, taps, group, unroll), out_...  14 us
    pallas_call x1, Pallas kernels, on_device(): pl.pallas_call(functools.partial(combine_kernel, share, axes, n_sta, n_tm...  12.1 us
    unnamed x23, local copies, waits for them, and re-layouts  6.51 us

commit v1 on v0

v1 whole, which is shorter than its diff:
```python
import functools
import math

import jax
import jax.numpy as jnp
from jax import lax
from jax.experimental import pallas as pl
from jax.experimental.pallas import tpu as pltpu
from jax.sharding import PartitionSpec as P

SAMPLES = 3072

sharpness = 400.0
epsilon = 1e-06
LANES = 128


def trace_kernel(
    taps, group, unroll, n_sta, n_tmpl,
    shift_hbm, valid_hbm, hypo_hbm, place_hbm, x_hbm, w_hbm, out_ref,
    shift_ref, valid_ref, hypo_ref, place_ref, x_ref, w_ref,
    xs, xw, rn, ws, acc, scr, part_ref, held,
    sem_in, sem_x, send_a, recv_a, send_b, recv_b
):
    comps, stations, samples = x_ref.shape
    chunks, temps, chunk_rows = part_ref.shape[:3]
    sta, tmpl = lax.axis_index("sta"), lax.axis_index("tmpl")
    barrier = pltpu.get_barrier_semaphore()
    for axis, me, size in (("sta", sta, n_sta), ("tmpl", tmpl, n_tmpl)):
        for k in range(1, size):
            pl.semaphore_signal(
                barrier, inc=1, device_id={axis: lax.rem(me + k, size)},
                device_id_type=pl.DeviceIdType.MESH,
            )
    w_copy = pltpu.make_async_copy(w_hbm, w_ref, sem_in.at[0])
    w_copy.start()
    x_copies = []
    for g in range(stations // group):
        span = pl.ds(g * group, group)
        x_copies.append(
            pltpu.make_async_copy(x_hbm.at[:, span, :], x_ref.at[:, span, :], sem_x.at[g])
        )
        x_copies[-1].start()
    small = []
    for n, (src, dst) in enumerate(
        (
            (shift_hbm, shift_ref), (valid_hbm, valid_ref),
            (hypo_hbm, hypo_ref), (place_hbm, place_ref),
        )
    ):
        small.append(pltpu.make_async_copy(src, dst, sem_in.at[n + 1]))
        small[-1].start()
    out_rows = acc.shape[1]
    rows = samples // LANES
    prows = -(-(rows + 1) // 8) * 8
    srows = comps * prows
    j_id = lax.broadcasted_iota(jnp.int32, (LANES, LANES), 0)
    i_id = lax.broadcasted_iota(jnp.int32, (LANES, LANES), 1)
    upper = j_id >= i_id
    gap = j_id - i_id
    band = jnp.concatenate(
        [
            jnp.where((gap >= 0) & (gap < taps), 1.0, 0.0),
            jnp.where(gap + LANES < taps, 1.0, 0.0),
        ],
        axis=0,
    ).astype(jnp.bfloat16)

    k_id = lax.broadcasted_iota(jnp.int32, (taps, LANES), 0)
    l_id = lax.broadcasted_iota(jnp.int32, (taps, LANES), 1)
    turn = jnp.where(lax.bitwise_and(k_id + l_id, LANES - 1) == 0, 1.0, 0.0).astype(jnp.bfloat16)
    w_copy.wait()
    for c in range(comps):
        for t in range(temps):
            wide = w_ref[t, c].astype(jnp.float32)
            power = jnp.sum(wide * wide, axis=-1, keepdims=True) / taps
            normed = (wide / (taps * jnp.sqrt(power + epsilon))).astype(jnp.bfloat16)
            ws[pl.ds((c * temps + t) * stations, stations), :] = jnp.dot(
                normed, turn, preferred_element_type=jnp.float32
            )

    xs[pl.ds(stations * srows, 8), :] = jnp.zeros((8, LANES), jnp.float32)

    def prepare(g, _):
        base = g * (group * srows)
        first = g * group
        for k in range(group * comps):
            xs[pl.ds(base + k * prows + prows - 8, 8), :] = jnp.zeros((8, LANES), jnp.float32)
        for c in range(comps):
            wave = x_ref[c, pl.ds(first, group), :].astype(jnp.float32)
            for r in range(rows):
                xs[pl.ds(base + c * prows + r, group, stride=srows), :] = wave[
                    :, r * LANES : (r + 1) * LANES
                ]
        count = group * srows
        here = xs[pl.ds(base, count), :]
        after = xs[pl.ds(base + 1, count), :]
        window = jnp.concatenate([here, after], axis=1)
        xw[pl.ds(base, count), :] = window.astype(jnp.bfloat16)
        square = window * window
        high = square.astype(jnp.bfloat16)
        low = (square - high.astype(jnp.float32)).astype(jnp.bfloat16)
        energy = jnp.dot(high, band, preferred_element_type=jnp.float32) + jnp.dot(
            low, band, preferred_element_type=jnp.float32
        )
        rn[pl.ds(base, count), :] = lax.rsqrt(energy * (1.0 / taps) + epsilon)
        return 0

    for g, copy in enumerate(x_copies):
        copy.wait()
        prepare(g, 0)
    for copy in small:
        copy.wait()

    lane = lax.broadcasted_iota(jnp.int32, (out_rows, LANES), 1)

    def one_station(s, slot, counts):
        sums = [None] * temps
        counts = list(counts)
        for c in range(comps):
            base = pl.multiple_of((s * comps + c) * prows, 16)
            data = xw[pl.ds(base, prows), :]
            inverse = rn[pl.ds(base, prows), :]
            tiles = []
            for t in range(temps):
                valid = valid_ref[c, t, s]
                counts[t] = counts[t] + valid
                row = ws[pl.ds((c * temps + t) * stations + s, 1), :] * valid.astype(jnp.float32)
                ring = pltpu.roll(
                    jnp.broadcast_to(row, (LANES, LANES)), 0, 1, stride=1, stride_axis=0
                )
                tiles.append(
                    jnp.concatenate(
                        [jnp.where(upper, ring, 0.0), jnp.where(upper, 0.0, ring)], axis=0
                    ).astype(jnp.bfloat16)
                )
            raw = jnp.dot(
                data, jnp.concatenate(tiles, axis=1), preferred_element_type=jnp.float32
            )
            for t in range(temps):
                term = raw[:, t * LANES : (t + 1) * LANES] * inverse
                sums[t] = term if sums[t] is None else sums[t] + term
        for t in range(temps):
            shift = shift_ref[t, s]
            whole = lax.shift_right_logical(shift, 7)
            part = lax.bitwise_and(shift, LANES - 1)
            scr[slot, t] = pltpu.roll(
                sums[t], lax.bitwise_and(LANES - part, LANES - 1), 1
            )
            near = scr[slot, t, pl.ds(whole, out_rows), :]
            far = scr[slot, t, pl.ds(whole + 1, out_rows), :]
            acc[t] += jnp.where(lane < LANES - part, near, far)
        return tuple(counts)

    acc[...] = jnp.zeros_like(acc)

    def some_stations(g, counts):
        for k in range(unroll):
            counts = one_station(g * unroll + k, k, counts)
        return counts

    counts = lax.fori_loop(
        0, stations // unroll, some_stations, tuple(jnp.int32(0) for _ in range(temps))
    )

    share = out_rows // chunks
    axes, hypos = place_ref.shape
    h_id = lax.broadcasted_iota(jnp.int32, (axes, hypos), 1)
    row_id = lax.broadcasted_iota(jnp.int32, (axes, LANES), 0)
    col_id = lax.broadcasted_iota(jnp.int32, (axes, LANES), 1)
    for t in range(temps):
        place = jnp.sum(
            jnp.where(h_id == hypo_ref[t], place_ref[...], 0.0), axis=1, keepdims=True
        )
        place_row = jnp.sum(jnp.where(row_id == col_id, place, 0.0), axis=0, keepdims=True)
        count_row = jnp.full((1, LANES), counts[t].astype(jnp.float32))
        for b in range(chunks):
            part_ref[b, t, pl.ds(0, share), :] = acc[t, pl.ds(b * share, share), :]
            part_ref[b, t, pl.ds(share, 1), :] = count_row
            part_ref[b, t, pl.ds(share + 1, 1), :] = place_row
            if chunk_rows > share + 2:
                part_ref[b, t, pl.ds(share + 2, chunk_rows - share - 2), :] = jnp.zeros(
                    (chunk_rows - share - 2, LANES), jnp.float32
                )

    pl.semaphore_wait(barrier, n_sta + n_tmpl - 2)
    copies = []
    for k in range(1, n_sta):
        peer = lax.rem(sta + k, n_sta)
        copies.append(
            pltpu.make_async_remote_copy(
                src_ref=part_ref.at[peer],
                dst_ref=held.at[k - 1],
                send_sem=send_a.at[k - 1],
                recv_sem=recv_a.at[k - 1],
                device_id={"sta": peer},
                device_id_type=pl.DeviceIdType.MESH,
            )
        )
        copies[-1].start()
    own = part_ref[sta]
    whole = own
    for k, copy in enumerate(copies):
        copy.wait_recv()
        whole = whole + held[k]
    row_id = lax.broadcasted_iota(jnp.int32, whole.shape, 1)
    out_ref[0] = jnp.where(
        row_id < share, sharpness * (whole / whole[:, share : share + 1, :]), own
    )
    later = []
    for k in range(1, n_tmpl):
        later.append(
            pltpu.make_async_remote_copy(
                src_ref=out_ref.at[0],
                dst_ref=out_ref.at[k],
                send_sem=send_b.at[k - 1],
                recv_sem=recv_b.at[k - 1],
                device_id={"tmpl": lax.rem(tmpl + k, n_tmpl)},
                device_id_type=pl.DeviceIdType.MESH,
            )
        )
        later[-1].start()
    for copy in copies:
        copy.wait_send()
    for copy in later:
        copy.wait()


def all_scores(records, templates, channel_valid, shifts, hypo_id, hypo_xyz):
    stations, comps, samples = records.shape
    temps, taps = templates.shape[0], templates.shape[-1]
    rows = samples // LANES
    prows = -(-(rows + 1) // 8) * 8
    total = stations * comps * prows
    group = math.gcd(stations, 16)
    unroll = math.gcd(stations, 2)
    n_sta, n_tmpl = lax.axis_size("sta"), lax.axis_size("tmpl")
    out_rows = SAMPLES // LANES
    chunk_rows = -(-(out_rows // n_sta + 2) // 8) * 8
    axes, hypos = hypo_xyz.shape
    block = (temps, chunk_rows, LANES)
    return pl.pallas_call(
        functools.partial(trace_kernel, taps, group, unroll, n_sta, n_tmpl),
        out_shape=jax.ShapeDtypeStruct((n_tmpl,) + block, jnp.float32),
        in_specs=[pl.BlockSpec(memory_space=pltpu.HBM)] * 6,
        out_specs=pl.BlockSpec(memory_space=pltpu.VMEM),
        scratch_shapes=[
            pltpu.SMEM((temps, stations), jnp.int32),
            pltpu.SMEM((comps, temps, stations), jnp.int32),
            pltpu.SMEM((temps,), jnp.int32),
            pltpu.VMEM((axes, hypos), jnp.float32),
            pltpu.VMEM((comps, stations, samples), jnp.bfloat16),
            pltpu.VMEM((temps, comps, stations, taps), jnp.bfloat16),
            pltpu.VMEM((total + 8, LANES), jnp.float32),
            pltpu.VMEM((total, 2 * LANES), jnp.bfloat16),
            pltpu.VMEM((total, LANES), jnp.float32),
            pltpu.VMEM((comps * temps * stations, LANES), jnp.float32),
            pltpu.VMEM((temps, out_rows, LANES), jnp.float32),
            pltpu.VMEM((unroll, temps, prows, LANES), jnp.float32),
            pltpu.VMEM((n_sta,) + block, jnp.float32),
            pltpu.VMEM((n_sta - 1,) + block, jnp.float32),
            pltpu.SemaphoreType.DMA((5,)),
            pltpu.SemaphoreType.DMA((stations // group,)),
            pltpu.SemaphoreType.DMA((n_sta - 1,)),
            pltpu.SemaphoreType.DMA((n_sta - 1,)),
            pltpu.SemaphoreType.DMA((n_tmpl - 1,)),
            pltpu.SemaphoreType.DMA((n_tmpl - 1,)),
        ],
        compiler_params=pltpu.CompilerParams(
            vmem_limit_bytes=60 * 2**20, collective_id=0, has_side_effects=True
        ),
        name="traces",
    )(
        shifts,
        jnp.transpose(channel_valid, (2, 0, 1)),
        hypo_id,
        hypo_xyz,
        jnp.transpose(records, (1, 0, 2)),
        jnp.transpose(templates, (0, 2, 1, 3)),
    )


def finish_kernel(
    share, axes, score_ref, best_hbm, evidence_hbm, place_hbm,
    best_ref, evidence_ref, place_ref, sem
):
    groups, temps = score_ref.shape[:2]
    pieces = [score_ref[n, t] for n in range(groups) for t in range(temps)]
    best = pieces[0]
    for piece in pieces[1:]:
        best = jnp.maximum(best, piece)
    best_ref[...] = best[:share]
    copies = [pltpu.make_async_copy(best_ref, best_hbm, sem.at[0])]
    copies[-1].start()
    total = jnp.zeros_like(best)
    sums = [jnp.zeros_like(best) for _ in range(axes)]
    for piece in pieces:
        weight = jnp.exp(piece - best)
        total = total + weight
        for j in range(axes):
            sums[j] = sums[j] + weight * piece[share + 1 : share + 2, j : j + 1]
    evidence_ref[...] = (best + jnp.log(total))[:share]
    copies.append(pltpu.make_async_copy(evidence_ref, evidence_hbm, sem.at[1]))
    copies[-1].start()
    for j in range(axes):
        located = sums[j] / total
        for r in range(share):
            place_ref[pl.ds(j, 1), pl.ds(r * LANES, LANES)] = located[r : r + 1]
    copies.append(pltpu.make_async_copy(place_ref, place_hbm, sem.at[2]))
    copies[-1].start()
    for copy in copies:
        copy.wait()


def on_device(records, templates, channel_valid, shifts, hypo_id, hypo_xyz):
    scores = all_scores(records, templates, channel_valid, shifts, hypo_id, hypo_xyz)
    axes = hypo_xyz.shape[0]
    share = SAMPLES // LANES // lax.axis_size("sta")
    hbm = pl.BlockSpec(memory_space=pltpu.HBM)
    shapes = ((share, LANES), (share, LANES), (axes, share * LANES))
    best, evidence, location = pl.pallas_call(
        functools.partial(finish_kernel, share, axes),
        out_shape=tuple(jax.ShapeDtypeStruct(shape, jnp.float32) for shape in shapes),
        in_specs=[pl.BlockSpec(memory_space=pltpu.VMEM)],
        out_specs=(hbm, hbm, hbm),
        scratch_shapes=[pltpu.VMEM(shape, jnp.float32) for shape in shapes]
        + [pltpu.SemaphoreType.DMA((3,))],
        name="finish",
    )(scores)
    return (best.reshape(-1), evidence.reshape(-1), location)


def solution(mesh):
    return jax.shard_map(
        on_device,
        mesh=mesh,
        in_specs=(
            P(("win", "sta"), None, None),
            P(("win", "tmpl"), "sta", None, None),
            P(("win", "tmpl"), "sta", None),
            P(("win", "tmpl"), "sta"),
            P(("win", "tmpl")),
            P(),
        ),
        out_specs=(P(("win", "sta")), P(("win", "sta")), P(None, ("win", "sta"))),
        check_vma=False,
    )
```

time: 33.7 us -> 28.1 us (0.83)
  local copies, waits for them, and re-layouts: 6.51 us -> 0 us
  Pallas kernels: 26.1 us -> 27.2 us
    unnamed x23 -> x0, local copies, waits for them, and re-layouts: 6.51 us -> none
    pallas_call x2, Pallas kernels: 26.1 us -> 27.2 us  [the longest x1 25.7 us: all_scores(): pl.pallas_call(functools.partial(trace_kernel, taps, group, unroll, n_sta...]
where the time goes in v1:
time: 28.1 us; the launch traced here: 27.9 us
  Pallas kernels  27.2 us (97%)
  between operations  0.64 us (2%)
    pallas_call x1, Pallas kernels, all_scores(): pl.pallas_call(functools.partial(trace_kernel, taps, group, unroll, n_sta...  25.7 us
    pallas_call x1, Pallas kernels, on_device(): pl.pallas_call(functools.partial(finish_kernel, share, axes), out_shape=t...  1.51 us

profile of v1, /device:TPU:0, one launch (start us, length us, event | category | flops | bytes accessed | tf_op | source)
XLA Modules:
  0.0 27.9 jit_solution(5700278590513597924)
XLA Ops:
  0.6 25.7 %traces.1.score_ref = f32[4,2,8,128]{3,2,1,0:T(8,128)} custom-call(s32[2,48]{1,0:T(2,128)} %shift_hbm.1, s32[3,2,48]{2,1,0:T(2,128)} %bitcast.7, s32[2]{0:T(128)} %hypo_hbm.1, f32[3,256]{1,0:T(4,128)} %place_hbm.1, bf16[3,48,3584]{2,1,0:T(8,128)(2,1)} %bitcast.5, bf16[2,3,48,100]{3,2,1,0:T(8,128)(2,1)} %bitcast.6), custom_call_target="tpu_custom_call" | custom-call | tf_op jit(solution)/shard_map/traces/pallas_call | solution.py:242
  26.4 1.5 %finish.1 = (f32[6,128]{1,0:T(8,128)}, f32[6,128]{1,0:T(8,128)}, f32[3,768]{1,0:T(4,128)}) custom-call(f32[4,2,8,128]{3,2,1,0:T(8,128)} %traces.1.score_ref), custom_call_target="tpu_custom_call" | custom-call | tf_op jit(solution)/shard_map/finish/pallas_call | solution.py:321

commit v2 on v1

--- a/solution.py
+++ b/solution.py
@@ -13,10 +13,11 @@
 sharpness = 400.0
 epsilon = 1e-06
 LANES = 128
+HALF = 64
 
 
 def trace_kernel(
-    taps, group, unroll, n_sta, n_tmpl,
+    taps, group, chans, unroll, n_sta, n_tmpl,
     shift_hbm, valid_hbm, hypo_hbm, place_hbm, x_hbm, w_hbm, out_ref,
     shift_ref, valid_ref, hypo_ref, place_ref, x_ref, w_ref,
     xs, xw, rn, ws, acc, scr, part_ref, held,
@@ -56,7 +57,6 @@
     srows = comps * prows
     j_id = lax.broadcasted_iota(jnp.int32, (LANES, LANES), 0)
     i_id = lax.broadcasted_iota(jnp.int32, (LANES, LANES), 1)
-    upper = j_id >= i_id
     gap = j_id - i_id
     band = jnp.concatenate(
         [
@@ -68,7 +68,12 @@
 
     k_id = lax.broadcasted_iota(jnp.int32, (taps, LANES), 0)
     l_id = lax.broadcasted_iota(jnp.int32, (taps, LANES), 1)
-    turn = jnp.where(lax.bitwise_and(k_id + l_id, LANES - 1) == 0, 1.0, 0.0).astype(jnp.bfloat16)
+    turns = [
+        jnp.where(
+            lax.bitwise_and(k_id + l_id - first, LANES - 1) == 0, 1.0, 0.0
+        ).astype(jnp.bfloat16)
+        for first in (0, HALF)
+    ]
     w_copy.wait()
     for c in range(comps):
         for t in range(temps):
@@ -76,76 +81,106 @@
             power = jnp.sum(wide * wide, axis=-1, keepdims=True) / taps
             normed = (wide / (taps * jnp.sqrt(power + epsilon))).astype(jnp.bfloat16)
             ws[pl.ds((c * temps + t) * stations, stations), :] = jnp.dot(
-                normed, turn, preferred_element_type=jnp.float32
+                normed, turns[t % 2], preferred_element_type=jnp.float32
             )
 
     xs[pl.ds(stations * srows, 8), :] = jnp.zeros((8, LANES), jnp.float32)
 
-    def prepare(g, _):
+    def spread(g):
         base = g * (group * srows)
-        first = g * group
         for k in range(group * comps):
             xs[pl.ds(base + k * prows + prows - 8, 8), :] = jnp.zeros((8, LANES), jnp.float32)
         for c in range(comps):
-            wave = x_ref[c, pl.ds(first, group), :].astype(jnp.float32)
+            wave = x_ref[c, pl.ds(g * group, group), :].astype(jnp.float32)
             for r in range(rows):
                 xs[pl.ds(base + c * prows + r, group, stride=srows), :] = wave[
                     :, r * LANES : (r + 1) * LANES
                 ]
-        count = group * srows
-        here = xs[pl.ds(base, count), :]
-        after = xs[pl.ds(base + 1, count), :]
+
+    def prepare(g, _):
+        base = pl.multiple_of(g * (chans * prows), 8)
+        mine = pl.ds(g * chans, chans)
+        here = xs[pl.ds(base, chans * prows), :]
+        after = xs[pl.ds(base + 1, chans * prows), :]
+        left = lax.broadcasted_iota(jnp.int32, here.shape, 1) < HALF
+        here_half = pltpu.roll(here, HALF, 1)
+        after_half = pltpu.roll(after, HALF, 1)
         window = jnp.concatenate([here, after], axis=1)
-        xw[pl.ds(base, count), :] = window.astype(jnp.bfloat16)
+        middle = jnp.concatenate([jnp.where(left, here_half, after_half), after_half], axis=1)
+        xw[mine, pl.ds(0, prows), :] = window.astype(jnp.bfloat16).reshape(chans, prows, -1)
+        xw[mine, pl.ds(prows, prows), :] = middle.astype(jnp.bfloat16).reshape(chans, prows, -1)
         square = window * window
         high = square.astype(jnp.bfloat16)
         low = (square - high.astype(jnp.float32)).astype(jnp.bfloat16)
         energy = jnp.dot(high, band, preferred_element_type=jnp.float32) + jnp.dot(
             low, band, preferred_element_type=jnp.float32
         )
-        rn[pl.ds(base, count), :] = lax.rsqrt(energy * (1.0 / taps) + epsilon)
+        inverse = lax.rsqrt(energy * (1.0 / taps) + epsilon)
+        swapped = pltpu.roll(inverse, HALF, 1)
+        rn[mine, pl.ds(0, prows), :] = jnp.where(left, inverse, swapped).reshape(
+            chans, prows, LANES
+        )
+        rn[mine, pl.ds(prows, prows), :] = jnp.where(left, swapped, inverse).reshape(
+            chans, prows, LANES
+        )
         return 0
 
     for g, copy in enumerate(x_copies):
         copy.wait()
-        prepare(g, 0)
+        spread(g)
+    lax.fori_loop(0, stations * comps // chans, prepare, 0)
     for copy in small:
         copy.wait()
 
     lane = lax.broadcasted_iota(jnp.int32, (out_rows, LANES), 1)
 
+    left = lax.broadcasted_iota(jnp.int32, (LANES, LANES), 1) < HALF
+    step = lax.bitwise_and(i_id, HALF - 1)
+    depth = -(-(taps + HALF - 1) // 16) * 16
+    rest = depth - LANES
+
     def one_station(s, slot, counts):
-        sums = [None] * temps
         counts = list(counts)
-        for c in range(comps):
-            base = pl.multiple_of((s * comps + c) * prows, 16)
-            data = xw[pl.ds(base, prows), :]
-            inverse = rn[pl.ds(base, prows), :]
-            tiles = []
-            for t in range(temps):
-                valid = valid_ref[c, t, s]
-                counts[t] = counts[t] + valid
-                row = ws[pl.ds((c * temps + t) * stations + s, 1), :] * valid.astype(jnp.float32)
-                ring = pltpu.roll(
-                    jnp.broadcast_to(row, (LANES, LANES)), 0, 1, stride=1, stride_axis=0
+        traces = []
+        for pair in range(temps // 2):
+            sums = None
+            for c in range(comps):
+                rings = []
+                for t in (2 * pair, 2 * pair + 1):
+                    valid = valid_ref[c, t, s]
+                    counts[t] = counts[t] + valid
+                    row = ws[pl.ds((c * temps + t) * stations + s, 1), :] * valid.astype(
+                        jnp.float32
+                    )
+                    rings.append(
+                        pltpu.roll(
+                            jnp.broadcast_to(row, (LANES, LANES)), 0, 1, stride=1, stride_axis=0
+                        )
+                    )
+                ring = jnp.where(left, rings[0], rings[1])
+                tile = jnp.concatenate(
+                    [
+                        jnp.where(j_id[:HALF] >= step[:HALF], ring[:HALF], 0.0),
+                        ring[HALF:],
+                        jnp.where(j_id[:rest] < step[:rest], ring[:rest], 0.0),
+                    ],
+                    axis=0,
+                ).astype(jnp.bfloat16)
+                raw = jnp.dot(
+                    xw[s * comps + c][:, :depth], tile, preferred_element_type=jnp.float32
                 )
-                tiles.append(
-                    jnp.concatenate(
-                        [jnp.where(upper, ring, 0.0), jnp.where(upper, 0.0, ring)], axis=0
-                    ).astype(jnp.bfloat16)
-                )
-            raw = jnp.dot(
-                data, jnp.concatenate(tiles, axis=1), preferred_element_type=jnp.float32
-            )
-            for t in range(temps):
-                term = raw[:, t * LANES : (t + 1) * LANES] * inverse
-                sums[t] = term if sums[t] is None else sums[t] + term
+                term = raw * rn[s * comps + c]
+                sums = term if sums is None else sums + term
+            low, high = sums[:prows], sums[prows:]
+            near = left[:prows]
+            traces.append(jnp.where(near, low, pltpu.roll(high, HALF, 1)))
+            traces.append(jnp.where(near, pltpu.roll(low, HALF, 1), high))
         for t in range(temps):
             shift = shift_ref[t, s]
             whole = lax.shift_right_logical(shift, 7)
             part = lax.bitwise_and(shift, LANES - 1)
             scr[slot, t] = pltpu.roll(
-                sums[t], lax.bitwise_and(LANES - part, LANES - 1), 1
+                traces[t], lax.bitwise_and(LANES - part, LANES - 1), 1
             )
             near = scr[slot, t, pl.ds(whole, out_rows), :]
             far = scr[slot, t, pl.ds(whole + 1, out_rows), :]
@@ -233,14 +268,16 @@
     prows = -(-(rows + 1) // 8) * 8
     total = stations * comps * prows
     group = math.gcd(stations, 16)
+    chans = math.gcd(stations, 4) * comps
     unroll = math.gcd(stations, 2)
+    assert temps % 2 == 0 and LANES - HALF + 1 < taps < LANES
     n_sta, n_tmpl = lax.axis_size("sta"), lax.axis_size("tmpl")
     out_rows = SAMPLES // LANES
     chunk_rows = -(-(out_rows // n_sta + 2) // 8) * 8
     axes, hypos = hypo_xyz.shape
     block = (temps, chunk_rows, LANES)
     return pl.pallas_call(
-        functools.partial(trace_kernel, taps, group, unroll, n_sta, n_tmpl),
+        functools.partial(trace_kernel, taps, group, chans, unroll, n_sta, n_tmpl),
         out_shape=jax.ShapeDtypeStruct((n_tmpl,) + block, jnp.float32),
         in_specs=[pl.BlockSpec(memory_space=pltpu.HBM)] * 6,
         out_specs=pl.BlockSpec(memory_space=pltpu.VMEM),
@@ -252,8 +289,8 @@
             pltpu.VMEM((comps, stations, samples), jnp.bfloat16),
             pltpu.VMEM((temps, comps, stations, taps), jnp.bfloat16),
             pltpu.VMEM((total + 8, LANES), jnp.float32),
-            pltpu.VMEM((total, 2 * LANES), jnp.bfloat16),
-            pltpu.VMEM((total, LANES), jnp.float32),
+            pltpu.VMEM((stations * comps, 2 * prows, 2 * LANES), jnp.bfloat16),
+            pltpu.VMEM((stations * comps, 2 * prows, LANES), jnp.float32),
             pltpu.VMEM((comps * temps * stations, LANES), jnp.float32),
             pltpu.VMEM((temps, out_rows, LANES), jnp.float32),
             pltpu.VMEM((unroll, temps, prows, LANES), jnp.float32),

time: 28.1 us -> 32.2 us (1.15)
  Pallas kernels: 27.2 us -> 31.4 us
    pallas_call x1, Pallas kernels: 25.7 us -> 29.9 us  [all_scores(): pl.pallas_call(functools.partial(trace_kernel, taps, group, chans, unroll...]
where the time goes in v2:
time: 32.2 us; the launch traced here: 32 us
  Pallas kernels  31.4 us (98%)
  between operations  0.64 us (2%)
    pallas_call x1, Pallas kernels, all_scores(): pl.pallas_call(functools.partial(trace_kernel, taps, group, chans, unroll...  29.9 us
    pallas_call x1, Pallas kernels, on_device(): pl.pallas_call(functools.partial(finish_kernel, share, axes), out_shape=t...  1.51 us

profile of v2, /device:TPU:0, one launch (start us, length us, event | category | flops | bytes accessed | tf_op | source)
XLA Modules:
  0.0 32.0 jit_solution(7686201677814288813)
XLA Ops:
  0.6 29.9 %traces.1.score_ref = f32[4,2,8,128]{3,2,1,0:T(8,128)} custom-call(s32[2,48]{1,0:T(2,128)} %shift_hbm.1, s32[3,2,48]{2,1,0:T(2,128)} %bitcast.7, s32[2]{0:T(128)} %hypo_hbm.1, f32[3,256]{1,0:T(4,128)} %place_hbm.1, bf16[3,48,3584]{2,1,0:T(8,128)(2,1)} %bitcast.5, bf16[2,3,48,100]{3,2,1,0:T(8,128)(2,1)} %bitcast.6), custom_call_target="tpu_custom_call" | custom-call | tf_op jit(solution)/shard_map/traces/pallas_call | solution.py:279
  30.5 1.5 %finish.1 = (f32[6,128]{1,0:T(8,128)}, f32[6,128]{1,0:T(8,128)}, f32[3,768]{1,0:T(4,128)}) custom-call(f32[4,2,8,128]{3,2,1,0:T(8,128)} %traces.1.score_ref), custom_call_target="tpu_custom_call" | custom-call | tf_op jit(solution)/shard_map/finish/pallas_call | solution.py:358

commit v3 on v1

--- a/solution.py
+++ b/solution.py
@@ -114,9 +114,9 @@
 
     lane = lax.broadcasted_iota(jnp.int32, (out_rows, LANES), 1)
 
-    def one_station(s, slot, counts):
+    def one_station(s, slot, counts, moved):
         sums = [None] * temps
-        counts = list(counts)
+        counts, moved = list(counts), list(moved)
         for c in range(comps):
             base = pl.multiple_of((s * comps + c) * prows, 16)
             data = xw[pl.ds(base, prows), :]
@@ -149,15 +149,18 @@
             )
             near = scr[slot, t, pl.ds(whole, out_rows), :]
             far = scr[slot, t, pl.ds(whole + 1, out_rows), :]
-            acc[t] += jnp.where(lane < LANES - part, near, far)
+            moved[t] = moved[t] + jnp.where(lane < LANES - part, near, far)
+        return counts, moved
+
+    acc[...] = jnp.zeros_like(acc)
+
+    def some_stations(g, counts):
+        moved = [acc[t] for t in range(temps)]
+        for k in range(unroll):
+            counts, moved = one_station(g * unroll + k, k, counts, moved)
+        for t in range(temps):
+            acc[t] = moved[t]
         return tuple(counts)
-
-    acc[...] = jnp.zeros_like(acc)
-
-    def some_stations(g, counts):
-        for k in range(unroll):
-            counts = one_station(g * unroll + k, k, counts)
-        return counts
 
     counts = lax.fori_loop(
         0, stations // unroll, some_stations, tuple(jnp.int32(0) for _ in range(temps))
@@ -233,7 +236,7 @@
     prows = -(-(rows + 1) // 8) * 8
     total = stations * comps * prows
     group = math.gcd(stations, 16)
-    unroll = math.gcd(stations, 2)
+    unroll = math.gcd(stations, 6)
     n_sta, n_tmpl = lax.axis_size("sta"), lax.axis_size("tmpl")
     out_rows = SAMPLES // LANES
     chunk_rows = -(-(out_rows // n_sta + 2) // 8) * 8

time: 28.1 us -> 23.4 us (0.83)
  Pallas kernels: 27.2 us -> 22.6 us
    pallas_call x1, Pallas kernels: 25.7 us -> 21.1 us  [all_scores(): pl.pallas_call(functools.partial(trace_kernel, taps, group, unroll, n_sta...]
where the time goes in v3:
time: 23.4 us; the launch traced here: 23.2 us
  Pallas kernels  22.6 us (97%)
  between operations  0.64 us (3%)
    pallas_call x1, Pallas kernels, all_scores(): pl.pallas_call(functools.partial(trace_kernel, taps, group, unroll, n_sta...  21.1 us
    pallas_call x1, Pallas kernels, on_device(): pl.pallas_call(functools.partial(finish_kernel, share, axes), out_shape=t...  1.51 us

profile of v3, /device:TPU:0, one launch (start us, length us, event | category | flops | bytes accessed | tf_op | source)
XLA Modules:
  0.0 23.2 jit_solution(6743605376002766671)
XLA Ops:
  0.6 21.1 %traces.1.score_ref = f32[4,2,8,128]{3,2,1,0:T(8,128)} custom-call(s32[2,48]{1,0:T(2,128)} %shift_hbm.1, s32[3,2,48]{2,1,0:T(2,128)} %bitcast.7, s32[2]{0:T(128)} %hypo_hbm.1, f32[3,256]{1,0:T(4,128)} %place_hbm.1, bf16[3,48,3584]{2,1,0:T(8,128)(2,1)} %bitcast.5, bf16[2,3,48,100]{3,2,1,0:T(8,128)(2,1)} %bitcast.6), custom_call_target="tpu_custom_call" | custom-call | tf_op jit(solution)/shard_map/traces/pallas_call | solution.py:245
  21.7 1.5 %finish.1 = (f32[6,128]{1,0:T(8,128)}, f32[6,128]{1,0:T(8,128)}, f32[3,768]{1,0:T(4,128)}) custom-call(f32[4,2,8,128]{3,2,1,0:T(8,128)} %traces.1.score_ref), custom_call_target="tpu_custom_call" | custom-call | tf_op jit(solution)/shard_map/finish/pallas_call | solution.py:324

commit v4 on v3

--- a/solution.py
+++ b/solution.py
@@ -63,8 +63,9 @@
             jnp.where((gap >= 0) & (gap < taps), 1.0, 0.0),
             jnp.where(gap + LANES < taps, 1.0, 0.0),
         ],
-        axis=0,
-    ).astype(jnp.bfloat16)
+        axis=1,
+    )
+    band = jnp.concatenate([band, band], axis=0).astype(jnp.bfloat16)
 
     k_id = lax.broadcasted_iota(jnp.int32, (taps, LANES), 0)
     l_id = lax.broadcasted_iota(jnp.int32, (taps, LANES), 1)
@@ -97,12 +98,13 @@
         after = xs[pl.ds(base + 1, count), :]
         window = jnp.concatenate([here, after], axis=1)
         xw[pl.ds(base, count), :] = window.astype(jnp.bfloat16)
-        square = window * window
+        square = here * here
         high = square.astype(jnp.bfloat16)
         low = (square - high.astype(jnp.float32)).astype(jnp.bfloat16)
-        energy = jnp.dot(high, band, preferred_element_type=jnp.float32) + jnp.dot(
-            low, band, preferred_element_type=jnp.float32
-        )
+        both = jnp.dot(
+            jnp.concatenate([high, low], axis=1), band, preferred_element_type=jnp.float32
+        )
+        energy = both[:, :LANES] + pltpu.roll(both[:, LANES:], count - 1, 0)
         rn[pl.ds(base, count), :] = lax.rsqrt(energy * (1.0 / taps) + epsilon)
         return 0
 
@@ -236,7 +238,7 @@
     prows = -(-(rows + 1) // 8) * 8
     total = stations * comps * prows
     group = math.gcd(stations, 16)
-    unroll = math.gcd(stations, 6)
+    unroll = math.gcd(stations, 12)
     n_sta, n_tmpl = lax.axis_size("sta"), lax.axis_size("tmpl")
     out_rows = SAMPLES // LANES
     chunk_rows = -(-(out_rows // n_sta + 2) // 8) * 8

time: 23.4 us -> 21.3 us (0.910)
  Pallas kernels: 22.6 us -> 20.5 us
    pallas_call x1, Pallas kernels: 21.1 us -> 19 us  [all_scores(): pl.pallas_call(functools.partial(trace_kernel, taps, group, unroll, n_sta...]
where the time goes in v4:
time: 21.3 us; the launch traced here: 21.1 us
  Pallas kernels  20.5 us (96%)
  between operations  0.64 us (3%)
    pallas_call x1, Pallas kernels, all_scores(): pl.pallas_call(functools.partial(trace_kernel, taps, group, unroll, n_sta...  19 us
    pallas_call x1, Pallas kernels, on_device(): pl.pallas_call(functools.partial(finish_kernel, share, axes), out_shape=t...  1.51 us

profile of v4, /device:TPU:0, one launch (start us, length us, event | category | flops | bytes accessed | tf_op | source)
XLA Modules:
  0.0 21.1 jit_solution(16190997397431896228)
XLA Ops:
  0.6 19.0 %traces.1.score_ref = f32[4,2,8,128]{3,2,1,0:T(8,128)} custom-call(s32[2,48]{1,0:T(2,128)} %shift_hbm.1, s32[3,2,48]{2,1,0:T(2,128)} %bitcast.7, s32[2]{0:T(128)} %hypo_hbm.1, f32[3,256]{1,0:T(4,128)} %place_hbm.1, bf16[3,48,3584]{2,1,0:T(8,128)(2,1)} %bitcast.5, bf16[2,3,48,100]{3,2,1,0:T(8,128)(2,1)} %bitcast.6), custom_call_target="tpu_custom_call" | custom-call | tf_op jit(solution)/shard_map/traces/pallas_call | solution.py:247
  19.6 1.5 %finish.1 = (f32[6,128]{1,0:T(8,128)}, f32[6,128]{1,0:T(8,128)}, f32[3,768]{1,0:T(4,128)}) custom-call(f32[4,2,8,128]{3,2,1,0:T(8,128)} %traces.1.score_ref), custom_call_target="tpu_custom_call" | custom-call | tf_op jit(solution)/shard_map/finish/pallas_call | solution.py:326

commit v5 on v4

--- a/solution.py
+++ b/solution.py
@@ -56,7 +56,8 @@
     srows = comps * prows
     j_id = lax.broadcasted_iota(jnp.int32, (LANES, LANES), 0)
     i_id = lax.broadcasted_iota(jnp.int32, (LANES, LANES), 1)
-    upper = j_id >= i_id
+    upper = jnp.where(j_id >= i_id, 1.0, 0.0).astype(jnp.bfloat16)
+    lower = jnp.where(j_id < i_id, 1.0, 0.0).astype(jnp.bfloat16)
     gap = j_id - i_id
     band = jnp.concatenate(
         [
@@ -130,12 +131,8 @@
                 row = ws[pl.ds((c * temps + t) * stations + s, 1), :] * valid.astype(jnp.float32)
                 ring = pltpu.roll(
                     jnp.broadcast_to(row, (LANES, LANES)), 0, 1, stride=1, stride_axis=0
-                )
-                tiles.append(
-                    jnp.concatenate(
-                        [jnp.where(upper, ring, 0.0), jnp.where(upper, 0.0, ring)], axis=0
-                    ).astype(jnp.bfloat16)
-                )
+                ).astype(jnp.bfloat16)
+                tiles.append(jnp.concatenate([ring * upper, ring * lower], axis=0))
             raw = jnp.dot(
                 data, jnp.concatenate(tiles, axis=1), preferred_element_type=jnp.float32
             )
@@ -238,7 +235,7 @@
     prows = -(-(rows + 1) // 8) * 8
     total = stations * comps * prows
     group = math.gcd(stations, 16)
-    unroll = math.gcd(stations, 12)
+    unroll = math.gcd(stations, 16)
     n_sta, n_tmpl = lax.axis_size("sta"), lax.axis_size("tmpl")
     out_rows = SAMPLES // LANES
     chunk_rows = -(-(out_rows // n_sta + 2) // 8) * 8

time: 21.3 us -> 21.3 us (level)
  no operation moved by 1% of the time
where the time goes in v5:
time: 21.3 us; the launch traced here: 21.1 us
  Pallas kernels  20.4 us (96%)
  between operations  0.64 us (3%)
    pallas_call x1, Pallas kernels, all_scores(): pl.pallas_call(functools.partial(trace_kernel, taps, group, unroll, n_sta...  18.9 us
    pallas_call x1, Pallas kernels, on_device(): pl.pallas_call(functools.partial(finish_kernel, share, axes), out_shape=t...  1.51 us

profile of v5, /device:TPU:0, one launch (start us, length us, event | category | flops | bytes accessed | tf_op | source)
XLA Modules:
  0.0 21.1 jit_solution(1437594622861244032)
XLA Ops:
  0.6 18.9 %traces.1.score_ref = f32[4,2,8,128]{3,2,1,0:T(8,128)} custom-call(s32[2,48]{1,0:T(2,128)} %shift_hbm.1, s32[3,2,48]{2,1,0:T(2,128)} %bitcast.7, s32[2]{0:T(128)} %hypo_hbm.1, f32[3,256]{1,0:T(4,128)} %place_hbm.1, bf16[3,48,3584]{2,1,0:T(8,128)(2,1)} %bitcast.5, bf16[2,3,48,100]{3,2,1,0:T(8,128)(2,1)} %bitcast.6), custom_call_target="tpu_custom_call" | custom-call | tf_op jit(solution)/shard_map/traces/pallas_call | solution.py:244
  19.6 1.5 %finish.1 = (f32[6,128]{1,0:T(8,128)}, f32[6,128]{1,0:T(8,128)}, f32[3,768]{1,0:T(4,128)}) custom-call(f32[4,2,8,128]{3,2,1,0:T(8,128)} %traces.1.score_ref), custom_call_target="tpu_custom_call" | custom-call | tf_op jit(solution)/shard_map/finish/pallas_call | solution.py:323
